TPU v7x, 256 devices: a whole 4x4x8 slice. The times are simulated.
256 devices in a mesh: scen: 16 (over z_hi, y, core), grp: 16 (over x, z_lo).
Axes of the slice: x: 4, y: 4, z: 8 (z_hi: 2, z_lo: 4; z = z_hi * 4 + z_lo), core: 2. Of those that a mesh axis runs over, the one named last changes fastest.
Arguments:
- linking: bfloat16 [32, 1024, 4096], P('scen', None, 'grp'), may hold values from -6 to 6
- reach_count: int32 [32], P('scen'), may hold values from 1 to 4, as said below
- diag_inverse: bfloat16 [32, 4, 256, 256], P('scen', None, 'grp'), as said below
- off_blocks: bfloat16 [32, 4, 2, 256, 256], P('scen', None, None, 'grp'), may hold values from -0.1875 to 0.1875
- targets: int32 [32, 4, 2], P('scen'), may hold values from 1 to 4, as said below
Outputs:
- schur: float32 [4096, 4096], P('grp', 'scen')
Inputs may be any that keep to these rules, and one draw needn't show every extreme that they name: Only the last reach_count[s] supernodes of scenario s take part; some scenario has all 4. `targets`: the 2 entries of row [s, j] are distinct supernodes above j, or 4 for an unused slot. `diag_inverse`: each block is lower triangular with a positive diagonal.
All inputs are finite; a program needn't handle non-finite values.
Results may differ from a plain program's by a relative error of at most 0.003.
Values may be sent and summed in bfloat16 or wider, within the bound.
A program may use at most 192 MiB of HBM per device.

v0:
```python
import math

import jax
import jax.numpy as jnp
from jax import lax
from jax.sharding import PartitionSpec as P


def local(linking, reach_count, diag_inverse, off_blocks, targets):
    local_scen = linking.shape[0]
    width = linking.shape[2]
    nodes = diag_inverse.shape[1]
    block = diag_inverse.shape[3]
    fan = off_blocks.shape[2]
    group = lax.axis_size("grp")
    full_width = width * group
    node_ids = jnp.arange(nodes, dtype=jnp.int32)
    stacked = jnp.concatenate([diag_inverse[:, :, None], off_blocks], axis=2)
    total = jnp.zeros((width, full_width), jnp.float32)
    for scenario in range(local_scen):
        first = nodes - reach_count[scenario]
        columns = linking[scenario].reshape(nodes, block, width)
        active = jnp.where((node_ids >= first)[:, None, None], columns, jnp.zeros_like(columns))
        all_panels = lax.all_gather(stacked[scenario], "grp", axis=2, tiled=True)
        pending = jnp.zeros((nodes, block, width), jnp.float32)
        solved_list = []
        for node in range(nodes):
            panel = all_panels[node]
            target_row = targets[scenario, node]

            def advance(pending_in, panel=panel, node=node, target_row=target_row):
                residual = (active[node].astype(jnp.float32) - pending_in[node]).astype(
                    jnp.bfloat16
                )
                solved_block = jnp.dot(
                    panel[0], residual, preferred_element_type=jnp.float32
                ).astype(jnp.bfloat16)
                for slot in range(fan):
                    update = jnp.dot(
                        panel[1 + slot], solved_block, preferred_element_type=jnp.float32
                    )
                    match = node_ids == target_row[slot]
                    pending_in = pending_in + jnp.where(
                        match[:, None, None], update[None], jnp.zeros_like(update)[None]
                    )
                return (solved_block, pending_in)

            solved_block, pending = advance(pending)
            solved_list.append(solved_block)
        solved = jnp.concatenate(solved_list, axis=0)

        def gram_piece(piece, solved=solved, first=first):
            return lax.dot_general(
                solved, piece, (((0,), (0,)), ((), ())), preferred_element_type=jnp.float32
            )

        def schur_rows(piece, start, gram_piece=gram_piece):
            return gram_piece(piece)

        total = total + schur_rows(lax.all_gather(solved, "grp", axis=1, tiled=True), jnp.int32(0))
    scaling = 1.0 / math.sqrt(local_scen * lax.axis_size("scen") * nodes * block)
    tiles = lax.psum_scatter(total, "scen", scatter_dimension=1, tiled=True)
    return tiles * scaling


def solution(mesh):
    return jax.shard_map(
        local,
        mesh=mesh,
        in_specs=(
            P("scen", None, "grp"),
            P("scen"),
            P("scen", None, "grp", None),
            P("scen", None, None, "grp", None),
            P("scen", None, None),
        ),
        out_specs=P("grp", "scen"),
        check_vma=False,
    )
```

profile of v0, /device:TPU:5, one launch (start us, length us, event | category | flops | bytes accessed | tf_op | source)
XLA Modules:
  0.0 679.9 jit_solution(16181762314322222687)
XLA Ops:
  6.5 0.0 all-gather.11.cloned.1.call-start
  6.5 1.6 pad_maximum_fusion.2
  8.1 0.0 all-gather.11.cloned.1.call-update
  8.2 0.0 all-gather.13.cloned.1.call-start
  8.2 0.7 all-gather.13.cloned.1.call-update
  8.9 0.0 all-gather.7.cloned.1.call-start
  9.0 1.3 fusion.54
  10.3 0.6 fusion.56
  11.4 0.0 copy-done.2
  11.4 0.7 fusion.55
  12.1 0.6 iota_compare_fusion.7
  12.7 0.6 slice.306
  13.4 0.5 iota_compare_fusion.8
  13.9 0.6 slice.304
  14.5 0.1 broadcast_select_fusion.1
  14.6 1.2 iota_compare_fusion.11
  15.8 1.2 iota_compare_fusion.9
  17.0 62.3 %all-gather.11.cloned.1.call-done = bf16[1,4,3,256,256]{4,3,2,1,0:T(8,128)(2,1)} async-done(((bf16[1,4,3,16,256]{4,3,2,1,0:T(8,128)(2,1)}), bf16[1,4,3,256,256]{4,3,2,1,0:T(8,128)(2,1)}) %all-gather.11.cloned.1.call-update) | async-done | bytes 1572880 | tf_op jit(solution)/shard_map/all_gather | solution.py:24
  79.3 1.2 convolution_convert_fusion.7
  80.5 1.1 fusion.43
  81.6 1.1 fusion.44
  82.7 0.2 select_add_fusion.3
  82.9 0.0 copy-done.1
  82.9 0.2 convolution_convert_fusion.6
  83.1 0.2 fusion.40
  83.2 0.2 fusion.41
  83.4 0.3 select_add_fusion.2
  83.7 0.2 convolution_convert_fusion.5
  83.9 0.2 fusion.37
  84.1 0.2 fusion.38
  84.3 1.4 convolution_convert_fusion.4
  85.7 0.9 pad_maximum_fusion
  86.6 0.0 all-gather.7.cloned.1.call-update
  86.6 0.0 all-gather.9.cloned.1.call-start
  87.2 0.7 iota_compare_fusion
  87.9 0.6 slice.325
  88.5 0.6 iota_compare_fusion.1
  89.1 0.6 slice.323
  89.8 1.2 iota_compare_fusion.4
  90.9 1.2 iota_compare_fusion.2
  92.2 0.1 broadcast_select_fusion
  92.3 72.6 %all-gather.13.cloned.1.call-done = bf16[1,4,3,256,256]{4,3,2,1,0:T(8,128)(2,1)} async-done(((bf16[1,4,3,16,256]{4,3,2,1,0:T(8,128)(2,1)}), bf16[1,4,3,256,256]{4,3,2,1,0:T(8,128)(2,1)}) %all-gather.13.cloned.1.call-update) | async-done | bytes 1572880 | tf_op jit(solution)/shard_map/all_gather | solution.py:24
  164.8 1.2 convolution_convert_fusion.3
  166.0 1.1 fusion.30
  167.1 1.1 fusion.31
  168.2 0.2 select_add_fusion.1
  168.4 0.2 convolution_convert_fusion.2
  168.6 0.2 fusion.27
  168.8 0.2 fusion.28
  169.0 0.3 select_add_fusion
  169.3 0.2 convolution_convert_fusion.1
  169.5 0.2 fusion.24
  169.7 0.2 fusion.25
  169.9 1.4 convolution_convert_fusion
  171.3 0.8 pad_maximum_fusion.1
  172.1 0.0 all-gather.9.cloned.1.call-update
  172.2 0.0 reduce-scatter.2.cloned.1.call-start
  172.2 195.2 %all-gather.7.cloned.1.call-done = bf16[1024,4096]{1,0:T(8,128)(2,1)} async-done(((bf16[1024,256]{1,0:T(8,128)(2,1)}), bf16[1024,4096]{1,0:T(8,128)(2,1)}) %all-gather.7.cloned.1.call-update) | async-done | bytes 8388624 | tf_op jit(solution)/shard_map/all_gather | solution.py:60
  367.4 7.7 %fusion.53 = f32[256,4096]{1,0:T(8,128)} fusion(bf16[1024,4096]{1,0:T(8,128)(2,1)} %all-gather.7.cloned.1.call-done, bf16[256,256]{1,0:T(8,128)(2,1)S(1)} %convolution_convert_fusion.4, bf16[256,256]{1,0:T(8,128)(2,1)S(1)} %convolution_convert_fusion.5, bf16[256,256]{1,0:T(8,128)(2,1)S(1)} %convolution_convert_fusion.6, ...), kind=kOutput, calls=%fused_computation.110 | convolution fusion | flops 2149580800 | bytes 13107200 | tf_op jit(solution)/shard_map/dot_general | solution.py:53
  375.1 181.4 %all-gather.9.cloned.1.call-done = bf16[1024,4096]{1,0:T(8,128)(2,1)} async-done(((bf16[1024,256]{1,0:T(8,128)(2,1)}), bf16[1024,4096]{1,0:T(8,128)(2,1)}) %all-gather.9.cloned.1.call-update) | async-done | bytes 8388624 | tf_op jit(solution)/shard_map/all_gather | solution.py:60
  556.5 8.9 %convolution_add_fusion = f32[256,4096]{1,0:T(8,128)} fusion(f32[256,4096]{1,0:T(8,128)} %fusion.53, bf16[1024,4096]{1,0:T(8,128)(2,1)} %all-gather.9.cloned.1.call-done, bf16[256,256]{1,0:T(8,128)(2,1)S(1)} %convolution_convert_fusion, bf16[256,256]{1,0:T(8,128)(2,1)S(1)} %convolution_convert_fusion.1, bf16[256,256]{1,0:T(8,128)(2,1)S(1)} %convolution_convert_fusion.2, ...), kind=kOutput, calls=%fused_computation | convolution fusion | flops 2150629376 | bytes 17301504 | tf_op jit(solution)/shard_map/dot_general | solution.py:53
  565.4 0.0 reduce-scatter.2.cloned.1.call-update
  565.4 106.3 %reduce-scatter.2.cloned.1.call-done = f32[256,256]{1,0:T(8,128)} async-done(((f32[256,4096]{1,0:T(8,128)}), f32[256,256]{1,0:T(8,128)}) %reduce-scatter.2.cloned.1.call-update) | async-done | bytes 262160 | tf_op jit(solution)/shard_map/reduce_scatter | solution.py:62
  671.7 1.7 broadcast_multiply_fusion
  (8 shorter events, 0.0 us)
Async XLA Ops:
  6.5 3.7 copy-start.3
  6.5 4.9 copy-start.2
  6.5 72.7 %all-gather.11.cloned.1.call-start = ((), (), s32[]{:S(2)}) async-start(), calls=%async_computation.4 | async-start | bytes 1671168 | tf_op jit(solution)/shard_map/all_gather | solution.py:24
  8.2 156.7 %all-gather.13.cloned.1.call-start = ((), (), s32[]{:S(2)}) async-start(), calls=%async_computation.5 | async-start | bytes 1671168 | tf_op jit(solution)/shard_map/all_gather | solution.py:24
  8.9 358.5 %all-gather.7.cloned.1.call-start = ((), (), s32[]{:S(2)}) async-start(), calls=%async_computation.1 | async-start | bytes 8912896 | tf_op jit(solution)/shard_map/all_gather | solution.py:60
  79.3 3.6 copy-start.1
  86.6 469.9 %all-gather.9.cloned.1.call-start = ((), (), s32[]{:S(2)}) async-start(), calls=%async_computation.2 | async-start | bytes 8912896 | tf_op jit(solution)/shard_map/all_gather | solution.py:60
  164.8 3.6 copy-start
  172.2 499.6 %reduce-scatter.2.cloned.1.call-start = ((), (), s32[]{:S(2)}) async-start(), calls=%async_computation.3 | async-start | bytes 4456448 | tf_op jit(solution)/shard_map/reduce_scatter | solution.py:62
Sparse Core Ops, SparseCore 0:
  9.2 70.0 all-gather.10
  81.1 83.7 all-gather.12
  166.5 200.7 all-gather.6
  369.0 187.4 all-gather.8
  565.5 106.1 reduce-scatter.1
where the time goes:
time: 682 us; the launch traced here: 680 us
  waiting for transfers between devices  618 us (91%)
  matrix products  28.4 us (4%)
  between operations  14.6 us (2%)
  other arithmetic  13.4 us (2%)
    all_gather x2, waiting for transfers between devices, local(): lax.all_gather(solved, 'grp', axis=1, tiled=True)  377 us
    all_gather x2, waiting for transfers between devices, local(): all_panels = lax.all_gather(stacked[scenario], 'grp', axis=2, tiled=True)  135 us
    reduce_scatter x1, waiting for transfers between devices, local(): tiles = lax.psum_scatter(total, 'scen', scatter_dimension=1, tiled=True)  106 us
    dot_general x2, matrix products, gram_piece(): lax.dot_general(solved, piece, (((0,), (0,)), ((), ())), preferred_elemen...  16.6 us
  transfers between devices with their start and end apart: 5, of which 5 were waited for; matrix products, arithmetic and copies ran while one was open for 5% of the time, Pallas kernels for 0%

commit v1 on v0

v1 whole, which is shorter than its diff:
```python
import math

import jax
import jax.numpy as jnp
from jax import lax
from jax.experimental import pallas as pl
from jax.experimental.pallas import tpu as pltpu
from jax.sharding import PartitionSpec as P

F32 = jnp.float32
BF16 = jnp.bfloat16
MESH = pl.DeviceIdType.MESH

NX = 4
NZ = 4
NY = 4
SB = 256
NS = 4
ROWS = NS * SB
HALF = ROWS // 2
PACK = 9
REL = (0, 1, 3, 2)

BATCHES = (
    ((3, 0), (3, 1), (3, 2), (0, 0), (0, 1), (0, 2)),
    ((1, 0), (1, 1), (1, 2), (2, 0), (2, 1), (2, 2)),
    ((3, 3), (0, 3), (1, 3), (2, 3)),
)
STARTS = (0, 6, 12)
OTHERS = ((0,), (1, 2), (0, 1, 2))
WIDTH = ((0, 1, 2), (0, 1, 2), (3,))
TILES = 16


def send(src, dst, send_sem, recv_sem, device):
    pltpu.make_async_remote_copy(
        src_ref=src,
        dst_ref=dst,
        send_sem=send_sem,
        recv_sem=recv_sem,
        device_id=device,
        device_id_type=MESH,
    ).start()


def await_bytes(ref, sem):
    pltpu.make_async_copy(ref, ref, sem).wait()


def flag(condition):
    return jnp.where(condition, 1.0, 0.0).astype(F32)


def mm(a, b):
    return lax.dot_general(a, b, (((1,), (1,)), ((), ())), preferred_element_type=F32)


def kernel(
    scaling,
    targets_hbm,
    reach_hbm,
    linking_hbm,
    diag,
    off,
    out,
    targets,
    reach,
    linking,
    choice,
    factors,
    lower,
    columns,
    solved,
    raw_z,
    solved_z,
    partial,
    from_core,
    to_y,
    from_y,
    reduced,
    near_z,
    near_x,
    slices,
    final,
    in_s,
    fz_s,
    fz_r,
    fx_s,
    fx_r,
    ff_s,
    ff_r,
    sx_s,
    sx_r,
    zl_s,
    zl_r,
    c_s,
    c_r,
    y_s,
    y_r,
    nz_s,
    nz_r,
    nx_s,
    nx_r,
    fn_s,
    fn_r,
):
    s = lax.axis_index("scen")
    g = lax.axis_index("grp")
    x, z = g // NZ, g % NZ
    core, y, z_hi = s % 2, (s // 2) % NY, s // (2 * NY)
    right_x, left_x, far_x = (x + 1) % NX, (x + 3) % NX, (x + 2) % NX
    right = (s, right_x * NZ + z)
    left = (s, left_x * NZ + z)
    upper = z // 2
    places = (z + 1 - 2 * (z % 2), 2 - upper, 3 - 3 * upper, z)

    def at_x(i):
        return (x + REL[i]) % NX

    barrier = pltpu.get_barrier_semaphore()

    def greet(k, carry):
        pl.semaphore_signal(barrier, inc=1, device_id=((s + k) % 16, g), device_id_type=MESH)
        return carry

    lax.fori_loop(1, 16, greet, 0)
    for k in range(1, NZ):
        pl.semaphore_signal(barrier, inc=1, device_id=(s, x * NZ + (z + k) % NZ), device_id_type=MESH)
    for k in range(1, NX):
        pl.semaphore_signal(barrier, inc=1, device_id=(s, ((x + k) % NX) * NZ + z), device_id_type=MESH)

    fetches = [(targets_hbm, targets), (reach_hbm, reach)]
    for sc in range(2):
        fetches.append((off.at[sc, 2], choice.at[sc]))
        fetches.append((diag.at[sc], factors.at[sc, g, pl.ds(0, NS)]))
        for i in range(2):
            fetches.append((off.at[sc, i], factors.at[sc, g, pl.ds(NS + 2 * i, 2)]))
    fetches.append((linking_hbm, linking))
    copies = [pltpu.make_async_copy(a, b, in_s.at[n]) for n, (a, b) in enumerate(fetches)]
    for copy in copies:
        copy.start()
    for copy in copies[:-1]:
        copy.wait()
    for sc in range(2):
        first = choice[sc, 0].astype(F32) * flag(targets[sc, 0, 2] == 3)
        second = choice[sc, 1].astype(F32) * flag(targets[sc, 1, 2] == 3)
        factors[sc, g, 8] = (first + second).astype(BF16)

    pl.semaphore_wait(barrier, 21)

    def shard(sc, xx, k):
        return factors.at[sc, xx * NZ + (z + k) % NZ]

    def x_send(sc, k):
        piece = shard(sc, x, k)
        send(piece, piece, fx_s.at[sc, 0, k], fx_r.at[sc, 0, k], right)
        send(piece, piece, fx_s.at[sc, 1, k], fx_r.at[sc, 1, k], left)

    def goes_on(q):
        return ((q < z) & (z < NZ - 1), (q > z) & (z > 0))

    def z_take(sc, o):
        q = places[o]
        piece = factors.at[sc, x * NZ + q]
        await_bytes(piece, fz_r.at[sc, q])
        for onward, device in zip(goes_on(q), ((s, g + 1), (s, g - 1))):

            @pl.when(onward)
            def _(device=device):
                send(piece, piece, fz_s.at[sc, 2 + o], fz_r.at[sc, q], device)

        x_send(sc, (q + NZ - z) % NZ)

    def pass_right(sc, k):
        piece = shard(sc, left_x, k)
        await_bytes(piece, fx_r.at[sc, 0, k])
        send(piece, piece, ff_s.at[sc, 0, k], ff_r.at[sc, 0, k], right)

    def pass_left(sc, k):
        piece = shard(sc, right_x, k)
        await_bytes(piece, fx_r.at[sc, 1, k])
        send(piece, piece, ff_s.at[sc, 1, k], ff_r.at[sc, 1, k], left)

    def rest(sc):
        for k in (1, 2):
            await_bytes(shard(sc, left_x, k), fx_r.at[sc, 0, k])
            await_bytes(shard(sc, far_x, k), ff_r.at[sc, 1, k])
        for k in (0, 3):
            await_bytes(shard(sc, right_x, k), fx_r.at[sc, 1, k])
            await_bytes(shard(sc, far_x, k), ff_r.at[sc, 0, k])

    def z_send(sc):
        own = factors.at[sc, g]

        @pl.when(z < NZ - 1)
        def _():
            send(own, own, fz_s.at[sc, 0], fz_r.at[sc, z], (s, g + 1))

        @pl.when(z > 0)
        def _():
            send(own, own, fz_s.at[sc, 1], fz_r.at[sc, z], (s, g - 1))

        x_send(sc, 0)

    def prepare(sc):
        for i in range(3):
            for j in range(i + 1, NS):
                if i == 2:
                    block = factors[sc, :, 8].reshape(SB, SB)
                else:
                    block = jnp.zeros((SB, SB), BF16)
                    for p in range(2):
                        chosen = flag(targets[sc, p, i] == j).astype(BF16)
                        block = block + factors[sc, :, 4 + 2 * i + p].reshape(SB, SB) * chosen
                lower[sc, j - 1, :, i * SB : (i + 1) * SB] = block

    def solve(sc, source, target, own=False, after=None):
        for j in range(NS):
            if own and j == 1:
                prepare(sc)
            here = slice(j * SB, (j + 1) * SB)
            residual = source[:, here].astype(F32) * flag(j >= NS - reach[sc])
            if j:
                residual = residual - mm(target[:, : j * SB], lower[sc, j - 1, :, : j * SB])
            inverse = factors[sc, :, j].reshape(SB, SB)
            target[:, here] = mm(residual.astype(BF16), inverse).astype(BF16)
            if after is not None:
                after(j)

    def x_part(sc, i, form, first=0, count=SB):
        return solved.at[sc, i, pl.ds(first, count), pl.ds(form * HALF, HALF)]

    def solve_own(sc):
        def after(j):
            if j % 2:
                form = j // 2
                own = x_part(sc, 0, form)
                send(own, x_part(sc, 2, form), sx_s.at[sc, form, 0], sx_r.at[sc, form, 0], right)
                send(own, x_part(sc, 1, form), sx_s.at[sc, form, 1], sx_r.at[sc, form, 1], left)

        solve(sc, columns.at[sc], solved.at[sc, 0], True, after)

    def pass_x(sc, form):
        await_bytes(x_part(sc, 2, form), sx_r.at[sc, form, 0])
        send(
            x_part(sc, 2, form, 0, SB // 2),
            x_part(sc, 3, form, 0, SB // 2),
            sx_s.at[sc, form, 2],
            sx_r.at[sc, form, 2],
            right,
        )
        await_bytes(x_part(sc, 1, form), sx_r.at[sc, form, 1])
        send(
            x_part(sc, 1, form, SB // 2, SB // 2),
            x_part(sc, 3, form, SB // 2, SB // 2),
            sx_s.at[sc, form, 3],
            sx_r.at[sc, form, 3],
            left,
        )

    def far(sc, form):
        for n in range(2):
            await_bytes(x_part(sc, 3, form, n * (SB // 2), SB // 2), sx_r.at[sc, form, 2 + n])

    def z_half(ref, h):
        return ref.at[pl.ds(h * (SB // 2), SB // 2)]

    def start_z():
        for h in range(2):

            @pl.when(z < NZ - 1)
            def _(h=h):
                send(z_half(columns.at[0], h), z_half(raw_z.at[z], h), zl_s.at[0, 0, h], zl_r.at[0, 0, h], (s, g + 1))

            @pl.when(z > 0)
            def _(h=h):
                send(z_half(columns.at[1], h), z_half(raw_z.at[z], h), zl_s.at[1, 0, h], zl_r.at[1, 0, h], (s, g - 1))

    def pass_z(k):
        for h in range(2):

            @pl.when(z - k >= 0)
            def _(h=h):
                block = z_half(raw_z.at[z - k], h)
                await_bytes(block, zl_r.at[0, k - 1, h])
                if k < NZ - 1:

                    @pl.when(z < NZ - 1)
                    def _():
                        send(block, block, zl_s.at[0, k, h], zl_r.at[0, k, h], (s, g + 1))

            @pl.when(z + k <= NZ - 1)
            def _(h=h):
                block = z_half(raw_z.at[z + k], h)
                await_bytes(block, zl_r.at[1, k - 1, h])
                if k < NZ - 1:

                    @pl.when(z > 0)
                    def _():
                        send(block, block, zl_s.at[1, k, h], zl_r.at[1, k, h], (s, g - 1))

    def solve_z(o):
        sc = (1 - z % 2) if o == 0 else (1 - upper)
        solve(sc, raw_z.at[places[o]], solved_z.at[places[o]])

    z_send(0)
    z_send(1)
    copies[-1].wait()
    for sc in range(2):
        for j in range(NS):
            block = linking[sc, j * SB : (j + 1) * SB, :].astype(F32)
            columns[sc, :, j * SB : (j + 1) * SB] = block.T.astype(BF16)
    z_take(0, 0)
    pass_right(0, 0)
    pass_right(1, 0)
    z_take(1, 0)
    z_take(0, 1)
    z_take(1, 1)
    z_take(0, 2)
    z_take(1, 2)
    start_z()
    pass_left(0, 1)
    pass_left(0, 2)
    pass_right(0, 3)
    pass_left(1, 1)
    pass_right(1, 3)
    pass_left(1, 2)
    rest(0)
    solve_own(0)
    pass_z(1)
    rest(1)
    solve_own(1)

    def store(n, tile):
        partial[0, n] = tile[: SB // 2]
        partial[1, n] = tile[SB // 2 :]

    def wide(sc):
        return solved[sc, 0:3].reshape(3 * SB, ROWS)

    def store_wide(n, product, axis):
        for i in range(3):
            store(n + i, lax.slice_in_dim(product, i * SB, (i + 1) * SB, axis=axis))

    def pair(first):
        return solved_z[first : first + 2].reshape(2 * SB, ROWS)

    def gram(batch):
        near_below = z % 2 == 1
        below = upper == 1
        if batch == 0:
            store_wide(0, mm(solved[0, 0], wide(0)) + mm(solved[1, 0], wide(1)), 1)

            @pl.when(near_below)
            def _():
                store_wide(3, mm(solved_z[places[0]], wide(0)), 1)

            @pl.when(jnp.logical_not(near_below))
            def _():
                store_wide(3, mm(wide(1), solved_z[places[0]]), 0)
        elif batch == 1:
            @pl.when(below)
            def _():
                product = mm(pair(0), wide(0))
                store_wide(6, product[SB:], 1)
                store_wide(9, product[:SB], 1)

            @pl.when(jnp.logical_not(below))
            def _():
                product = mm(wide(1), pair(2))
                store_wide(6, product[:, :SB], 0)
                store_wide(9, product[:, SB:], 0)
        else:
            store(12, mm(solved[0, 0], solved[0, 3]) + mm(solved[1, 0], solved[1, 3]))

            @pl.when(near_below)
            def _():
                store(13, mm(solved_z[places[0]], solved[0, 3]))

            @pl.when(jnp.logical_not(near_below))
            def _():
                store(13, mm(solved[1, 3], solved_z[places[0]]))

            @pl.when(below)
            def _():
                product = mm(pair(0), solved[0, 3])
                store(14, product[SB:])
                store(15, product[:SB])

            @pl.when(jnp.logical_not(below))
            def _():
                product = mm(solved[1, 3], pair(2))
                store(14, product[:, :SB])
                store(15, product[:, SB:])

    def span(batch):
        return pl.ds(STARTS[batch], len(BATCHES[batch]))

    def to_core(batch):
        send(
            partial.at[1 - core, span(batch)],
            from_core.at[span(batch)],
            c_s.at[batch],
            c_r.at[batch],
            (s + 1 - 2 * core, g),
        )

    def of_y(yy, first=0, count=32):
        return pl.ds(pl.multiple_of((yy % NY) * 32 + first, 16), count)

    def both_cores(n, rows):
        return partial[core, n, rows, :] + from_core[n, rows, :]

    def over_tiles(batch, body):
        def step(n, carry):
            body(n)
            return carry

        lax.fori_loop(STARTS[batch], STARTS[batch] + len(BATCHES[batch]), step, 0)

    def along_y(batch):
        tiles = span(batch)
        await_bytes(from_core.at[tiles], c_r.at[batch])
        for k in (2, 1, 3):

            def body(n, k=k):
                to_y[k - 1, n] = both_cores(n, of_y(y + k)).astype(BF16)

            over_tiles(batch, body)
            send(
                to_y.at[k - 1, tiles],
                from_y.at[k - 1, tiles],
                y_s.at[batch, k - 1],
                y_r.at[batch, k - 1],
                (z_hi * 8 + ((y + k) % NY) * 2 + core, g),
            )

    def finish_y(batch):
        tiles = span(batch)
        for k in range(1, NY):
            await_bytes(from_y.at[k - 1, tiles], y_r.at[batch, k - 1])
        for n, (o, i) in enumerate(BATCHES[batch], STARTS[batch]):
            value = both_cores(n, of_y(y))
            for k in range(1, NY):
                value += from_y[k - 1, n].astype(F32)
            value = value.astype(BF16)
            if o == 3:
                slices[3, i] = value
            else:
                reduced[o, i] = value
                if i == 0:
                    near_x[0, o] = value

    def batch_z(ref, place, batch):
        return ref.at[place, pl.ds(WIDTH[batch][0], len(WIDTH[batch]))]

    def batch_x(ref, place, batch):
        return ref.at[place, pl.ds(OTHERS[batch][0], len(OTHERS[batch]))]

    def to_groups(batch):
        for o in OTHERS[batch]:
            send(
                batch_z(reduced, o, batch),
                batch_z(near_z, z, batch),
                nz_s.at[batch, o],
                nz_r.at[batch, z],
                (s, x * NZ + places[o]),
            )
        for i in WIDTH[batch]:
            if i:
                back = (0, 2, 1, 3)[i]
                send(
                    reduced.at[pl.ds(OTHERS[batch][0], len(OTHERS[batch])), i],
                    batch_x(near_x, back, batch),
                    nx_s.at[batch, i - 1],
                    nx_r.at[batch, back - 1],
                    (s, at_x(i) * NZ + z),
                )

    def from_groups(batch):
        for o in OTHERS[batch]:
            await_bytes(batch_z(near_z, places[o], batch), nz_r.at[batch, places[o]])
        for i in WIDTH[batch]:
            if i:
                await_bytes(batch_x(near_x, i, batch), nx_r.at[batch, i - 1])
        for o in OTHERS[batch]:
            for i in WIDTH[batch]:
                deliver(o, i)

    out_rows = pl.ds(pl.multiple_of(core * 128 + y * 32, 32), 32)

    def deliver(o, i):
        if o < 3:
            both = near_z[places[o], i].astype(F32) + near_x[i, o].astype(F32)
            slices[o, i] = both.astype(BF16)
        b = at_x(i) * NZ + places[o]
        piece = slices.at[o, i]
        target = final.at[z_hi, out_rows]

        @pl.when(b == s)
        def _():
            pltpu.make_async_copy(piece, target, fn_r.at[0]).start()

        @pl.when(b != s)
        def _():
            send(piece, target, fn_s.at[o * 4 + i], fn_r.at[0], (b, g))

    solve_z(0)
    pass_z(2)
    pass_x(0, 0)
    pass_x(0, 1)
    pass_x(1, 0)
    pass_x(1, 1)
    gram(0)
    to_core(0)
    solve_z(1)
    pass_z(3)
    along_y(0)
    solve_z(2)
    gram(1)
    to_core(1)
    far(0, 0)
    far(0, 1)
    along_y(1)
    far(1, 0)
    far(1, 1)
    gram(2)
    to_core(2)
    finish_y(0)
    to_groups(0)
    along_y(2)
    from_groups(0)
    finish_y(1)
    to_groups(1)
    finish_y(2)
    to_groups(2)
    for i in range(3):
        deliver(3, i)
    from_groups(1)
    deliver(3, 3)
    from_groups(2)

    for sc in range(2):

        @pl.when(z < NZ - 1)
        def _(sc=sc):
            await_bytes(factors.at[sc, g], fz_s.at[sc, 0])

        @pl.when(z > 0)
        def _(sc=sc):
            await_bytes(factors.at[sc, g], fz_s.at[sc, 1])

        for o in range(3):
            for onward in goes_on(places[o]):

                @pl.when(onward)
                def _(sc=sc, o=o):
                    await_bytes(factors.at[sc, g], fz_s.at[sc, 2 + o])

        for d in range(2):
            for k in range(4):
                await_bytes(factors.at[sc, g], fx_s.at[sc, d, k])
            for k in ((0, 3), (1, 2))[d]:
                await_bytes(factors.at[sc, g], ff_s.at[sc, d, k])
            for n in range(2):
                await_bytes(x_part(sc, 0, d), sx_s.at[sc, d, n])
                await_bytes(x_part(sc, 0, d, 0, SB // 2), sx_s.at[sc, d, 2 + n])
    for k in range(NZ - 1):

        @pl.when((z - k >= 0) & (z < NZ - 1))
        def _(k=k):
            for h in range(2):
                await_bytes(z_half(raw_z.at[0], h), zl_s.at[0, k, h])

        @pl.when((z + k <= NZ - 1) & (z > 0))
        def _(k=k):
            for h in range(2):
                await_bytes(z_half(raw_z.at[0], h), zl_s.at[1, k, h])

    for batch in range(3):
        await_bytes(from_core.at[span(batch)], c_s.at[batch])
    for batch in range(3):
        for k in range(NY - 1):
            await_bytes(from_y.at[k, span(batch)], y_s.at[batch, k])
    for batch in range(3):
        for o in OTHERS[batch]:
            await_bytes(batch_z(near_z, 0, batch), nz_s.at[batch, o])
        for i in WIDTH[batch]:
            if i:
                await_bytes(batch_x(near_x, 0, batch), nx_s.at[batch, i - 1])
    await_bytes(final, fn_r.at[0])

    @pl.when(z > s % NZ)
    def _():
        out[...] = ((final[0].astype(F32) + final[1].astype(F32)) * scaling).T

    @pl.when(z <= s % NZ)
    def _():
        out[...] = (final[0].astype(F32) + final[1].astype(F32)) * scaling

    for o in range(4):
        for i in range(4):

            @pl.when(at_x(i) * NZ + places[o] != s)
            def _(o=o, i=i):
                await_bytes(slices.at[0, 0], fn_s.at[o * 4 + i])


def local(linking, reach_count, diag_inverse, off_blocks, targets):
    scaling = 1.0 / math.sqrt(linking.shape[0] * 16 * ROWS)
    dma = pltpu.SemaphoreType.DMA
    vmem = pl.BlockSpec(memory_space=pltpu.VMEM)
    hbm = pl.BlockSpec(memory_space=pltpu.HBM)

    def body(*refs):
        kernel(scaling, *refs)

    operands = (jnp.swapaxes(targets, 1, 2), reach_count, linking, diag_inverse, off_blocks)
    return pl.pallas_call(
        body,
        out_shape=jax.ShapeDtypeStruct((SB, SB), F32),
        in_specs=[hbm] * 5,
        out_specs=vmem,
        scratch_shapes=[
            pltpu.SMEM((2, 2, NS), jnp.int32),
            pltpu.SMEM((2,), jnp.int32),
            pltpu.VMEM((2, ROWS, SB), BF16),
            pltpu.VMEM((2, 2, 16, SB), BF16),
            pltpu.VMEM((2, 16, PACK, 16, SB), BF16),
            pltpu.VMEM((2, NS - 1, SB, 3 * SB), BF16),
            pltpu.VMEM((2, SB, ROWS), BF16),
            pltpu.VMEM((2, NX, SB, ROWS), BF16),
            pltpu.VMEM((NZ, SB, ROWS), BF16),
            pltpu.VMEM((NZ, SB, ROWS), BF16),
            pltpu.VMEM((2, TILES, SB // 2, SB), F32),
            pltpu.VMEM((TILES, SB // 2, SB), F32),
            pltpu.VMEM((NY - 1, TILES, 32, SB), BF16),
            pltpu.VMEM((NY - 1, TILES, 32, SB), BF16),
            pltpu.VMEM((3, NX, 32, SB), BF16),
            pltpu.VMEM((NZ, NX, 32, SB), BF16),
            pltpu.VMEM((NX, 3, 32, SB), BF16),
            pltpu.VMEM((4, NX, 32, SB), BF16),
            pltpu.VMEM((2, SB, SB), BF16),
            dma((11,)),
            dma((2, 5)),
            dma((2, 4)),
            dma((2, 2, 4)),
            dma((2, 2, 4)),
            dma((2, 2, 4)),
            dma((2, 2, 4)),
            dma((2, 2, 4)),
            dma((2, 2, 4)),
            dma((2, 3, 2)),
            dma((2, 3, 2)),
            dma((3,)),
            dma((3,)),
            dma((3, 3)),
            dma((3, 3)),
            dma((3, 3)),
            dma((3, 4)),
            dma((3, 3)),
            dma((3, 3)),
            dma((16,)),
            dma((1,)),
        ],
        compiler_params=pltpu.CompilerParams(
            collective_id=0,
            has_side_effects=True,
            vmem_limit_bytes=44 * 1024 * 1024,
        ),
        cost_estimate=pl.CostEstimate(flops=3_000_000_000, bytes_accessed=5_000_000, transcendentals=0),
    )(*(pltpu.with_memory_space_constraint(a, pltpu.HBM) for a in operands))


def solution(mesh):
    return jax.shard_map(
        local,
        mesh=mesh,
        in_specs=(
            P("scen", None, "grp"),
            P("scen"),
            P("scen", None, "grp", None),
            P("scen", None, None, "grp", None),
            P("scen", None, None),
        ),
        out_specs=P("grp", "scen"),
        check_vma=False,
    )
```

time: 682 us -> 90.5 us (0.13)
  waiting for transfers between devices: 618 us -> 0 us
  Pallas kernels: 0 us -> 89.7 us
  matrix products: 28.4 us -> 0 us
  between operations: 14.6 us -> 0.01 us
  other arithmetic: 13.4 us -> 0 us
    all_gather x4 -> x0, waiting for transfers between devices: 511 us -> none  [the longest x2 377 us: local(): lax.all_gather(solved, 'grp', axis=1, tiled=True)]
    reduce_scatter x1 -> x0, waiting for transfers between devices: 106 us -> none  [local(): tiles = lax.psum_scatter(total, 'scen', scatter_dimension=1, tiled=True)]
    pallas_call x0 -> x1, Pallas kernels: none -> 89.7 us  [local(): pl.pallas_call(body, out_shape=jax.ShapeDtypeStruct((SB, SB), F32), in_sp...]
    dot_general x22 -> x0, matrix products: 28.4 us -> none  [the longest x2 16.6 us: gram_piece(): lax.dot_general(solved, piece, (((0,), (0,)), ((), ())), preferred_elemen...]
    eq x8 -> x0, other arithmetic: 7.27 us -> none  [advance(): match = node_ids == target_row[slot]]
  transfers between devices with their start and end apart: 5 -> 0, of which waited for: 5 -> 0; matrix products, arithmetic and copies ran while one was open for 5% -> 0% of each run, Pallas kernels for 0% -> 0%
where the time goes in v1:
time: 90.5 us; the launch traced here: 90.4 us
  Pallas kernels  89.7 us (99%)
    pallas_call x1, Pallas kernels, local(): pl.pallas_call(body, out_shape=jax.ShapeDtypeStruct((SB, SB), F32), in_sp...  89.7 us

profile of v1, /device:TPU:5, one launch (start us, length us, event | category | flops | bytes accessed | tf_op | source)
XLA Modules:
  0.0 90.4 jit_solution(1889895587776182190)
XLA Ops:
  0.0 89.7 %shard_map.55 = f32[256,256]{1,0:T(8,128)S(1)} custom-call(s32[2,2,4]{2,1,0:T(2,128)} %bitcast.1, s32[2]{0:T(128)} %refs_1_.1, bf16[2,1024,256]{2,1,0:T(8,128)(2,1)} %refs_2_.1, bf16[2,4,16,256]{3,2,1,0:T(8,128)(2,1)} %refs_3_.1, bf16[2,4,2,16,256]{4,3,2,1,0:T(8,128)(2,1)} %refs_4_.1), custom_call_target="tpu_custom_call" | custom-call | flops 3000000000 | bytes 5000000 | tf_op jit(solution)/shard_map/pallas_call | solution.py:619
  89.7 0.7 copy.7

commit v2 on v1

--- a/solution.py
+++ b/solution.py
@@ -311,19 +311,19 @@
             block = linking[sc, j * SB : (j + 1) * SB, :].astype(F32)
             columns[sc, :, j * SB : (j + 1) * SB] = block.T.astype(BF16)
     z_take(0, 0)
+    z_take(0, 1)
+    z_take(1, 0)
+    z_take(1, 1)
     pass_right(0, 0)
-    pass_right(1, 0)
-    z_take(1, 0)
-    z_take(0, 1)
-    z_take(1, 1)
     z_take(0, 2)
     z_take(1, 2)
     start_z()
     pass_left(0, 1)
     pass_left(0, 2)
     pass_right(0, 3)
+    pass_right(1, 3)
     pass_left(1, 1)
-    pass_right(1, 3)
+    pass_right(1, 0)
     pass_left(1, 2)
     rest(0)
     solve_own(0)
@@ -505,18 +505,18 @@
         def _():
             send(piece, target, fn_s.at[o * 4 + i], fn_r.at[0], (b, g))
 
+    pass_z(2)
     solve_z(0)
-    pass_z(2)
     pass_x(0, 0)
+    solve_z(1)
     pass_x(0, 1)
     pass_x(1, 0)
     pass_x(1, 1)
     gram(0)
     to_core(0)
-    solve_z(1)
     pass_z(3)
+    solve_z(2)
     along_y(0)
-    solve_z(2)
     gram(1)
     to_core(1)
     far(0, 0)
@@ -528,14 +528,14 @@
     to_core(2)
     finish_y(0)
     to_groups(0)
+    for i in range(3):
+        deliver(3, i)
     along_y(2)
     from_groups(0)
     finish_y(1)
     to_groups(1)
     finish_y(2)
     to_groups(2)
-    for i in range(3):
-        deliver(3, i)
     from_groups(1)
     deliver(3, 3)
     from_groups(2)

time: 90.5 us -> 89 us (0.983)
  Pallas kernels: 89.7 us -> 87.7 us
    pallas_call x1, Pallas kernels: 89.7 us -> 87.7 us  [local(): pl.pallas_call(body, out_shape=jax.ShapeDtypeStruct((SB, SB), F32), in_sp...]
where the time goes in v2:
time: 89 us; the launch traced here: 88.4 us
  Pallas kernels  87.7 us (99%)
    pallas_call x1, Pallas kernels, local(): pl.pallas_call(body, out_shape=jax.ShapeDtypeStruct((SB, SB), F32), in_sp...  87.7 us

profile of v2, /device:TPU:5, one launch (start us, length us, event | category | flops | bytes accessed | tf_op | source)
XLA Modules:
  0.0 88.4 jit_solution(7890875067551018097)
XLA Ops:
  0.0 87.7 %shard_map.55 = f32[256,256]{1,0:T(8,128)S(1)} custom-call(s32[2,2,4]{2,1,0:T(2,128)} %bitcast.1, s32[2]{0:T(128)} %refs_1_.1, bf16[2,1024,256]{2,1,0:T(8,128)(2,1)} %refs_2_.1, bf16[2,4,16,256]{3,2,1,0:T(8,128)(2,1)} %refs_3_.1, bf16[2,4,2,16,256]{4,3,2,1,0:T(8,128)(2,1)} %refs_4_.1), custom_call_target="tpu_custom_call" | custom-call | flops 3000000000 | bytes 5000000 | tf_op jit(solution)/shard_map/pallas_call | solution.py:619
  87.7 0.7 copy.7

commit v3 on v2

--- a/solution.py
+++ b/solution.py
@@ -531,9 +531,9 @@
     for i in range(3):
         deliver(3, i)
     along_y(2)
-    from_groups(0)
     finish_y(1)
     to_groups(1)
+    from_groups(0)
     finish_y(2)
     to_groups(2)
     from_groups(1)

time: 89 us -> 90 us (1.011)
  Pallas kernels: 87.7 us -> 89.2 us
    pallas_call x1, Pallas kernels: 87.7 us -> 89.2 us  [local(): pl.pallas_call(body, out_shape=jax.ShapeDtypeStruct((SB, SB), F32), in_sp...]
where the time goes in v3:
time: 90 us; the launch traced here: 89.9 us
  Pallas kernels  89.2 us (99%)
    pallas_call x1, Pallas kernels, local(): pl.pallas_call(body, out_shape=jax.ShapeDtypeStruct((SB, SB), F32), in_sp...  89.2 us

profile of v3, /device:TPU:5, one launch (start us, length us, event | category | flops | bytes accessed | tf_op | source)
XLA Modules:
  0.0 89.9 jit_solution(17235378622336015683)
XLA Ops:
  0.0 89.2 %shard_map.55 = f32[256,256]{1,0:T(8,128)S(1)} custom-call(s32[2,2,4]{2,1,0:T(2,128)} %bitcast.1, s32[2]{0:T(128)} %refs_1_.1, bf16[2,1024,256]{2,1,0:T(8,128)(2,1)} %refs_2_.1, bf16[2,4,16,256]{3,2,1,0:T(8,128)(2,1)} %refs_3_.1, bf16[2,4,2,16,256]{4,3,2,1,0:T(8,128)(2,1)} %refs_4_.1), custom_call_target="tpu_custom_call" | custom-call | flops 3000000000 | bytes 5000000 | tf_op jit(solution)/shard_map/pallas_call | solution.py:619
  89.2 0.7 copy.7

commit v4 on v2

--- a/solution.py
+++ b/solution.py
@@ -478,13 +478,12 @@
                 )
 
     def from_groups(batch):
-        for o in OTHERS[batch]:
-            await_bytes(batch_z(near_z, places[o], batch), nz_r.at[batch, places[o]])
-        for i in WIDTH[batch]:
+        for n, i in enumerate(WIDTH[batch]):
             if i:
                 await_bytes(batch_x(near_x, i, batch), nx_r.at[batch, i - 1])
-        for o in OTHERS[batch]:
-            for i in WIDTH[batch]:
+            for o in OTHERS[batch]:
+                if n == 0:
+                    await_bytes(batch_z(near_z, places[o], batch), nz_r.at[batch, places[o]])
                 deliver(o, i)
 
     out_rows = pl.ds(pl.multiple_of(core * 128 + y * 32, 32), 32)

time: 89 us -> 88.6 us (level)
  no operation moved by 1% of the time
where the time goes in v4:
time: 88.6 us; the launch traced here: 88 us
  Pallas kernels  87.3 us (99%)
    pallas_call x1, Pallas kernels, local(): pl.pallas_call(body, out_shape=jax.ShapeDtypeStruct((SB, SB), F32), in_sp...  87.3 us

profile of v4, /device:TPU:5, one launch (start us, length us, event | category | flops | bytes accessed | tf_op | source)
XLA Modules:
  0.0 88.0 jit_solution(9669252420705364115)
XLA Ops:
  0.0 87.3 %shard_map.55 = f32[256,256]{1,0:T(8,128)S(1)} custom-call(s32[2,2,4]{2,1,0:T(2,128)} %bitcast.1, s32[2]{0:T(128)} %refs_1_.1, bf16[2,1024,256]{2,1,0:T(8,128)(2,1)} %refs_2_.1, bf16[2,4,16,256]{3,2,1,0:T(8,128)(2,1)} %refs_3_.1, bf16[2,4,2,16,256]{4,3,2,1,0:T(8,128)(2,1)} %refs_4_.1), custom_call_target="tpu_custom_call" | custom-call | flops 3000000000 | bytes 5000000 | tf_op jit(solution)/shard_map/pallas_call | solution.py:618
  87.3 0.7 copy.7

commit v5 on v4

--- a/solution.py
+++ b/solution.py
@@ -521,14 +521,14 @@
     far(0, 0)
     far(0, 1)
     along_y(1)
+    finish_y(0)
+    to_groups(0)
+    for i in range(3):
+        deliver(3, i)
     far(1, 0)
     far(1, 1)
     gram(2)
     to_core(2)
-    finish_y(0)
-    to_groups(0)
-    for i in range(3):
-        deliver(3, i)
     along_y(2)
     from_groups(0)
     finish_y(1)

time: 88.6 us -> 88.6 us (level)
  no operation moved by 1% of the time
where the time goes in v5:
time: 88.6 us; the launch traced here: 88.5 us
  Pallas kernels  87.7 us (99%)
    pallas_call x1, Pallas kernels, local(): pl.pallas_call(body, out_shape=jax.ShapeDtypeStruct((SB, SB), F32), in_sp...  87.7 us

profile of v5, /device:TPU:5, one launch (start us, length us, event | category | flops | bytes accessed | tf_op | source)
XLA Modules:
  0.0 88.5 jit_solution(6212575564715644842)
XLA Ops:
  0.0 87.7 %shard_map.55 = f32[256,256]{1,0:T(8,128)S(1)} custom-call(s32[2,2,4]{2,1,0:T(2,128)} %bitcast.1, s32[2]{0:T(128)} %refs_1_.1, bf16[2,1024,256]{2,1,0:T(8,128)(2,1)} %refs_2_.1, bf16[2,4,16,256]{3,2,1,0:T(8,128)(2,1)} %refs_3_.1, bf16[2,4,2,16,256]{4,3,2,1,0:T(8,128)(2,1)} %refs_4_.1), custom_call_target="tpu_custom_call" | custom-call | flops 3000000000 | bytes 5000000 | tf_op jit(solution)/shard_map/pallas_call | solution.py:618
  87.8 0.7 copy.7

commit v6 on v4

--- a/solution.py
+++ b/solution.py
@@ -315,6 +315,7 @@
     z_take(1, 0)
     z_take(1, 1)
     pass_right(0, 0)
+    pass_right(1, 0)
     z_take(0, 2)
     z_take(1, 2)
     start_z()
@@ -323,7 +324,6 @@
     pass_right(0, 3)
     pass_right(1, 3)
     pass_left(1, 1)
-    pass_right(1, 0)
     pass_left(1, 2)
     rest(0)
     solve_own(0)

time: 88.6 us -> 90 us (1.016)
  Pallas kernels: 87.3 us -> 88.8 us
    pallas_call x1, Pallas kernels: 87.3 us -> 88.8 us  [local(): pl.pallas_call(body, out_shape=jax.ShapeDtypeStruct((SB, SB), F32), in_sp...]
where the time goes in v6:
time: 90 us; the launch traced here: 89.5 us
  Pallas kernels  88.8 us (99%)
    pallas_call x1, Pallas kernels, local(): pl.pallas_call(body, out_shape=jax.ShapeDtypeStruct((SB, SB), F32), in_sp...  88.8 us

profile of v6, /device:TPU:5, one launch (start us, length us, event | category | flops | bytes accessed | tf_op | source)
XLA Modules:
  0.0 89.5 jit_solution(2678033796810256216)
XLA Ops:
  0.0 88.8 %shard_map.55 = f32[256,256]{1,0:T(8,128)S(1)} custom-call(s32[2,2,4]{2,1,0:T(2,128)} %bitcast.1, s32[2]{0:T(128)} %refs_1_.1, bf16[2,1024,256]{2,1,0:T(8,128)(2,1)} %refs_2_.1, bf16[2,4,16,256]{3,2,1,0:T(8,128)(2,1)} %refs_3_.1, bf16[2,4,2,16,256]{4,3,2,1,0:T(8,128)(2,1)} %refs_4_.1), custom_call_target="tpu_custom_call" | custom-call | flops 3000000000 | bytes 5000000 | tf_op jit(solution)/shard_map/pallas_call | solution.py:618
  88.8 0.7 copy.7

commit v7 on v4

--- a/solution.py
+++ b/solution.py
@@ -312,10 +312,10 @@
             columns[sc, :, j * SB : (j + 1) * SB] = block.T.astype(BF16)
     z_take(0, 0)
     z_take(0, 1)
+    pass_right(0, 0)
+    z_take(0, 2)
     z_take(1, 0)
     z_take(1, 1)
-    pass_right(0, 0)
-    z_take(0, 2)
     z_take(1, 2)
     start_z()
     pass_left(0, 1)

time: 88.6 us -> 90.8 us (1.025); the launches traced: 88 us -> 89.1 us
  Pallas kernels: 87.3 us -> 88.4 us
    pallas_call x1, Pallas kernels: 87.3 us -> 88.4 us  [local(): pl.pallas_call(body, out_shape=jax.ShapeDtypeStruct((SB, SB), F32), in_sp...]
where the time goes in v7:
time: 90.8 us; the launch traced here: 89.1 us
  Pallas kernels  88.4 us (97%)
    pallas_call x1, Pallas kernels, local(): pl.pallas_call(body, out_shape=jax.ShapeDtypeStruct((SB, SB), F32), in_sp...  88.4 us

profile of v7, /device:TPU:5, one launch (start us, length us, event | category | flops | bytes accessed | tf_op | source)
XLA Modules:
  0.0 89.1 jit_solution(15732025348158572663)
XLA Ops:
  0.0 88.4 %shard_map.55 = f32[256,256]{1,0:T(8,128)S(1)} custom-call(s32[2,2,4]{2,1,0:T(2,128)} %bitcast.1, s32[2]{0:T(128)} %refs_1_.1, bf16[2,1024,256]{2,1,0:T(8,128)(2,1)} %refs_2_.1, bf16[2,4,16,256]{3,2,1,0:T(8,128)(2,1)} %refs_3_.1, bf16[2,4,2,16,256]{4,3,2,1,0:T(8,128)(2,1)} %refs_4_.1), custom_call_target="tpu_custom_call" | custom-call | flops 3000000000 | bytes 5000000 | tf_op jit(solution)/shard_map/pallas_call | solution.py:618
  88.4 0.7 copy.7
